TPU v7x, 256 devices: a whole 4x4x8 slice. The times are simulated.
256 devices in a mesh: dp: 64 (over x, z, core), mp: 4 (over y).
Axes of the slice: x: 4, y: 4, z: 8, core: 2. Of those that a mesh axis runs over, the one named last changes fastest.
Arguments:
- activations: bfloat16 [32768, 2560], P('dp'), may hold values from -6 to 6
- cotangent: bfloat16 [32768, 6912], P('dp', 'mp'), may hold values from -6 to 6
- frozen_weight: bfloat16 [2560, 6912], P(None, 'mp'), may hold values from -0.078125 to 0.078125
- skew_params: bfloat16 [10, 256, 256], replicated, may hold values from -0.125 to 0.125
- tile_order: int32 [20], replicated, may hold values from 0 to 19, each once
- block_owner: int32 [10], replicated, may hold values from 0 to 63, as said below
Outputs:
- input_grad: bfloat16 [32768, 2560], P('dp', 'mp')
- skew_grads: float32 [192, 256, 256], P('dp')
Inputs may be any that keep to these rules, and one draw needn't show every extreme that they name: `tile_order`: a permutation of the 20 tiles. `block_owner`: no index of dp owns more than 3 blocks, and some index owns exactly 3; indices 0 and 64 - 1 own blocks in every draw.
All inputs are finite; a program needn't handle non-finite values.
Results may differ from a plain program's by a relative error of at most 0.001.
Values sent between devices are 32-bit elements; how exact they have to be, the bound alone decides.
No kernel may reach another device: no remote copies, remote signals or barrier semaphores. Data moves between devices by JAX's collectives and lax.ppermute only.
A program may use at most 128 MiB of HBM per device.

v0:
```python
import math
import jax
import jax.numpy as jnp
from jax import lax
from jax.sharding import PartitionSpec as P

SLOTS = 3
highest = lax.Precision.HIGHEST


def product(first, second):
    return jnp.einsum("bij,bjk->bik", first, second, precision=highest)


def cayley_parts(params):
    plain = params.astype(jnp.float32)
    skew = plain - jnp.swapaxes(plain, 1, 2)
    square = product(skew, skew)
    cube = product(square, skew)
    identity = jnp.eye(skew.shape[1], dtype=jnp.float32)
    return (skew, identity[None] + 2.0 * skew + 2.0 * square + cube)


def to_blocks(matrix, order, tile_count, block_count):
    tiled = matrix.reshape(matrix.shape[0], tile_count, -1)
    return jnp.take(tiled, order, axis=1).reshape(matrix.shape[0], block_count, -1)


def inverse_order(order, tile_count):
    positions = jnp.arange(tile_count, dtype=jnp.int32)
    matches = (order[:, None] == positions[None, :]).astype(jnp.int32)
    return jnp.sum(positions[:, None] * matches, axis=0)


def adjoint(gram, skew):
    transposed = jnp.swapaxes(skew, 1, 2)
    left = product(gram, transposed)
    right = product(transposed, gram)
    total = (
        2.0 * gram
        + 2.0 * (left + right)
        + product(left, transposed)
        + product(transposed, left)
        + product(transposed, right)
    )
    return total - jnp.swapaxes(total, 1, 2)


def local(activations, cotangent, frozen_weight, skew_params, tile_order, block_owner):
    token_rows = activations.shape[0]
    tile_count = tile_order.shape[0]
    block_count = block_owner.shape[0]
    skew, rotation = cayley_parts(skew_params)
    partial_grad = lax.dot_general(
        cotangent, frozen_weight, (((1,), (1,)), ((), ())), preferred_element_type=jnp.float32
    )
    feature_grad = lax.psum(partial_grad, "mp")
    grad_blocks = to_blocks(feature_grad, tile_order, tile_count, block_count)
    own_tiles = tile_count // lax.axis_size("mp")
    inverse = inverse_order(tile_order, tile_count)
    own_places = lax.dynamic_slice_in_dim(inverse, lax.axis_index("mp") * own_tiles, own_tiles, 0)
    half_rows = rotation.reshape(block_count * 2, rotation.shape[1] // 2, rotation.shape[2])
    own_rotation = jnp.take(half_rows, own_places, axis=0)
    own_blocks = jnp.take(grad_blocks, own_places // 2, axis=1)
    own_rotated = jnp.einsum("tkj,kij->tki", own_blocks, own_rotation, precision=highest)
    input_grad = own_rotated.reshape(token_rows, -1).astype(jnp.bfloat16)
    quarter = token_rows // lax.axis_size("mp")
    row_start = lax.axis_index("mp") * quarter
    some_inputs = lax.dynamic_slice_in_dim(activations, row_start, quarter, 0)
    input_blocks = to_blocks(some_inputs, tile_order, tile_count, block_count).astype(jnp.float32)
    some_grads = lax.dynamic_slice_in_dim(grad_blocks, row_start, quarter, 0)
    local_gram = jnp.einsum("tbi,tbj->bij", input_blocks, some_grads, precision=highest)
    gram = lax.psum(local_gram, ("dp", "mp"))
    owned = (block_owner == lax.axis_index("dp")).astype(jnp.int32)
    ranking = jnp.cumsum(owned) - 1
    slot_ids = jnp.arange(SLOTS, dtype=jnp.int32)
    selector = ((owned[None, :] == 1) & (ranking[None, :] == slot_ids[:, None])).astype(jnp.float32)
    gram_slots = jnp.einsum("sb,bij->sij", selector, gram, precision=highest)
    skew_slots = jnp.einsum("sb,bij->sij", selector, skew, precision=highest)
    scaling = 1.0 / math.sqrt(token_rows * lax.axis_size("dp"))
    skew_grads = adjoint(gram_slots, skew_slots) * scaling
    return (input_grad, skew_grads)


def solution(mesh):
    placed = (P("dp", None), P("dp", "mp"), P(None, "mp"), P(), P(), P())
    return jax.shard_map(
        local,
        mesh=mesh,
        in_specs=placed,
        out_specs=(P("dp", "mp"), P("dp", None, None)),
        check_vma=False,
    )
```

profile of v0, /device:TPU:2, one launch (start us, length us, event | category | flops | bytes accessed | tf_op | source)
XLA Modules:
  0.0 453.6 jit_solution(274264501818761207)
XLA Ops:
  7.2 0.0 copy-start
  7.2 0.0 all-reduce.3.cloned.1.call-start
  7.2 11.4 %fusion.34 = f32[512,2560]{0,1:T(8,128)} fusion(bf16[512,1728]{0,1:T(8,128)(2,1)} %param.7, bf16[2560,1728]{0,1:T(8,128)(2,1)} %param.8), kind=kOutput, calls=%fused_computation.62 | convolution fusion | flops 4529848320 | bytes 15859712 | tf_op jit(solution)/shard_map/dot_general | solution.py:54
  18.7 5.9 %copy.80 = f32[512,20,128]{2,0,1:T(8,128)} copy(f32[512,20,128]{0,2,1:T(8,128)} %bitcast.49) | data formatting | bytes 10485760 | tf_op jit(solution)/shard_map/reshape | solution.py:25
  24.6 0.0 copy-start.5
  24.6 0.0 copy-start.6
  24.6 0.0 all-reduce.3.cloned.1.call-update
  24.6 0.0 all-reduce.5.cloned.1.call-start
  24.7 0.6 copy-done.5
  25.3 0.2 reduce-window.8
  25.4 0.0 copy-done.6
  25.5 0.1 broadcast_in_dim.63
  25.5 0.1 broadcast_in_dim.64
  25.7 0.0 copy-done
  25.7 0.1 constant_dynamic-slice_fusion
  25.7 0.3 copy.100
  26.1 0.3 copy.84
  26.4 0.7 gather_fusion.3
  27.1 0.3 copy.85
  27.4 1.6 copy.77
  29.0 0.0 copy-start.4
  29.1 1.9 copy.78
  31.0 0.1 select_reduce_fusion
  31.1 0.1 compare_and_fusion.2
  31.2 0.0 copy-done.4
  31.2 0.5 bitcast_select_fusion
  31.7 2.4 bitcast_subtract_fusion
  34.1 3.9 fusion
  38.0 104.7 %all-reduce.3.cloned.1.call-done = f32[512,20,128]{2,0,1:T(8,128)} async-done(((f32[512,20,128]{2,0,1:T(8,128)}), f32[512,20,128]{2,0,1:T(8,128)}) %all-reduce.3.cloned.1.call-update) | async-done | bytes 5242896 | tf_op jit(solution)/shard_map/psum | solution.py:57
  142.7 5.7 %gather_fusion.1 = f32[20,512,128]{2,1,0:T(8,128)} fusion(f32[512,20,128]{2,0,1:T(8,128)} %all-reduce.3.cloned.1.call-done, s32[1024]{0:T(1024)S(1)} %pad_clamp_fusion.1), kind=kCustom, calls=%fused_computation.1 | custom fusion | bytes 10485840 | tf_op jit(solution)/shard_map/jit(_take)/gather | solution.py:26
  148.4 5.9 %copy.81 = f32[512,20,128]{0,2,1:T(8,128)} copy(f32[512,20,128]{2,0,1:T(8,128)} %bitcast.47) | data formatting | bytes 10485760 | tf_op jit(solution)/shard_map/jit(_take)/gather | solution.py:26
  154.3 5.9 %copy.82 = f32[512,10,256]{2,0,1:T(8,128)} copy(f32[512,10,256]{0,2,1:T(8,128)} %bitcast.48) | data formatting | bytes 10485760 | tf_op jit(solution)/shard_map/jit(_take)/gather | solution.py:26
  160.2 2.9 broadcast_select_fusion
  163.1 0.0 copy-start.2
  163.1 2.3 copy-done.2
  165.4 2.8 fusion.11
  168.2 0.0 all-reduce.5.cloned.1.call-update
  168.3 1.5 copy.90
  169.8 2.9 fusion.33
  172.7 4.8 %add_add_fusion = f32[10,256,256]{2,1,0:T(8,128)} fusion(f32[10,256,256]{2,1,0:T(8,128)S(1)} %fusion.33, f32[10,256,256]{2,1,0:T(8,128)S(1)} %bitcast_subtract_fusion, f32[256,256]{1,0:T(8,128)S(1)} %fusion.24), kind=kOutput, calls=%fused_computation.13 | convolution fusion | flops 2016542720 | bytes 8126464 | tf_op jit(solution)/shard_map/bij,bjk->bik/dot_general | solution.py:12
  177.4 3.2 gather_fusion
  180.6 3.2 gather_fusion.2
  183.8 4.7 %fusion.7 = bf16[5,128,512]{2,1,0:T(8,128)(2,1)} fusion(f32[5,512,256]{2,1,0:T(8,128)S(1)} %gather_fusion.2, pred[5]{0:T(512)(128)(4,1)S(1)} %get-tuple-element.16, f32[5,128,256]{2,1,0:T(8,128)} %gather_fusion, pred[5]{0:T(512)(128)(4,1)S(1)} %get-tuple-element.10), kind=kOutput, calls=%fused_computation.14 | convolution fusion | flops 1007779840 | bytes 3932170 | tf_op jit(solution)/shard_map/tkj,kij->tki/dot_general | solution.py:65
  188.5 2.2 copy.97
  190.7 0.0 copy-start.3
  190.7 240.4 %all-reduce.5.cloned.1.call-done = f32[10,256,256]{2,1,0:T(8,128)} async-done(((f32[10,256,256]{2,1,0:T(8,128)}), f32[10,256,256]{2,1,0:T(8,128)}) %all-reduce.5.cloned.1.call-update) | async-done | bytes 2621456 | tf_op jit(solution)/shard_map/psum | solution.py:73
  431.1 4.8 %fusion.2 = f32[3,256,256]{2,0,1:T(4,128)S(1)} fusion(f32[10,256,256]{2,1,0:T(8,128)} %all-reduce.5.cloned.1.call-done, s32[10]{0:T(128)S(1)} %add_bitcast_fusion, pred[10]{0:T(512)(128)(4,1)S(1)} %get-tuple-element.14), kind=kOutput, calls=%fused_computation.6 | convolution fusion | flops 23593020 | bytes 3407922 | tf_op jit(solution)/shard_map/sb,bij->sij/dot_general | solution.py:78
  436.0 0.0 copy-done.3
  436.0 1.0 fusion.17
  437.0 1.0 fusion.19
  438.0 1.1 convolution_add_fusion.2
  439.1 0.9 convolution_add_fusion.1
  440.1 0.0 copy-start.1
  440.1 1.8 convolution_add_fusion
  441.9 2.3 copy.96
  444.2 1.5 fusion.14
  445.6 1.1 copy.98
  446.8 0.0 copy-done.1
  (9 shorter events, 0.1 us)
Async XLA Ops:
  7.2 18.5 %copy-start = (bf16[512,2560]{1,0:T(8,128)(2,1)S(1)}, bf16[512,2560]{1,0:T(8,128)(2,1)}, u32[]{:S(2)}) copy-start(bf16[512,2560]{1,0:T(8,128)(2,1)} %param.6) | copy-start | bytes 7864324
  7.2 135.6 %all-reduce.3.cloned.1.call-start = ((), (), s32[]{:S(2)}) async-start(), calls=%async_computation | async-start | bytes 10485760 | tf_op jit(solution)/shard_map/psum | solution.py:57
  24.6 0.7 copy-start.5
  24.6 0.8 copy-start.6
  24.6 406.5 %all-reduce.5.cloned.1.call-start = ((), (), s32[]{:S(2)}) async-start(), calls=%async_computation.1 | async-start | bytes 5242880 | tf_op jit(solution)/shard_map/psum | solution.py:73
  29.0 2.1 copy-start.4
  163.1 2.3 copy-start.2
  190.7 245.2 %copy-start.3 = (f32[3,256,256]{2,0,1:T(4,128)S(1)}, f32[3,256,256]{2,0,1:T(4,128)}, u32[]{:S(2)}) copy-start(f32[3,256,256]{2,0,1:T(4,128)} %fusion) | copy-start | bytes 2359300
  440.1 6.7 %copy-start.1 = (bf16[512,2560]{1,0:T(8,128)(2,1)S(1)}, bf16[512,2560]{1,0:T(8,128)(2,1)}, u32[]{:S(2)}) copy-start(bf16[512,2560]{1,0:T(8,128)(2,1)} %param.6) | copy-start | bytes 7864324
Sparse Core Ops, SparseCore 0:
  24.7 117.9 all-reduce.2
  168.4 262.7 all-reduce.4
where the time goes:
time: 454 us
  waiting for transfers between devices  345 us (76%)
  local copies, waits for them, and re-layouts  45.2 us (10%)
  matrix products  41.2 us (9%)
  between operations  14.3 us (3%)
  other arithmetic  7.66 us (2%)
    psum x1, waiting for transfers between devices, local(): gram = lax.psum(local_gram, ('dp', 'mp'))  240 us
    psum x1, waiting for transfers between devices, local(): feature_grad = lax.psum(partial_grad, 'mp')  105 us
    gather x5, local copies, waits for them, and re-layouts, to_blocks(): jnp.take(tiled, order, axis=1).reshape(matrix.shape[0], block_count, -1)  18.5 us
    dot_general x7, matrix products, product(): return jnp.einsum('bij,bjk->bik', first, second, precision=highest)  13.5 us
    dot_general x1, matrix products, local(): lax.dot_general(cotangent, frozen_weight, (((1,), (1,)), ((), ())), prefe...  11.4 us
  transfers between devices with their start and end apart: 2, of which 2 were waited for; matrix products, arithmetic and copies ran while one was open for 8% of the time, Pallas kernels for 0%

commit v1 on v0

--- a/solution.py
+++ b/solution.py
@@ -54,7 +54,7 @@
     partial_grad = lax.dot_general(
         cotangent, frozen_weight, (((1,), (1,)), ((), ())), preferred_element_type=jnp.float32
     )
-    feature_grad = lax.psum(partial_grad, "mp")
+    feature_grad = jnp.sum(lax.all_gather(partial_grad, "mp"), axis=0)
     grad_blocks = to_blocks(feature_grad, tile_order, tile_count, block_count)
     own_tiles = tile_count // lax.axis_size("mp")
     inverse = inverse_order(tile_order, tile_count)

time: 454 us -> 549 us (1.21)
  waiting for transfers between devices: 345 us -> 421 us
  other arithmetic: 7.66 us -> 18.9 us
  local copies, waits for them, and re-layouts: 45.2 us -> 52.7 us
    all_gather x0 -> x1, waiting for transfers between devices: none -> 180 us  [local(): feature_grad = jnp.sum(lax.all_gather(partial_grad, 'mp'), axis=0)]
    psum x1 -> x0, waiting for transfers between devices: 105 us -> none  [local(): feature_grad = lax.psum(partial_grad, 'mp')]
    reduce_sum x0 -> x1, other arithmetic: none -> 11.2 us  [local(): feature_grad = jnp.sum(lax.all_gather(partial_grad, 'mp'), axis=0)]
    reduce_sum x0 -> x1, local copies, waits for them, and re-layouts: none -> 5.9 us  [local(): feature_grad = jnp.sum(lax.all_gather(partial_grad, 'mp'), axis=0)]
  transfers between devices with their start and end apart: 2 -> 2, of which waited for: 2 -> 2; matrix products, arithmetic and copies ran while one was open for 8% -> 7% of each run, Pallas kernels for 0% -> 0%
where the time goes in v1:
time: 549 us; the launch traced here: 548 us
  waiting for transfers between devices  421 us (77%)
  local copies, waits for them, and re-layouts  52.7 us (10%)
  matrix products  41.2 us (8%)
  other arithmetic  18.9 us (3%)
  between operations  14.3 us (3%)
    psum x1, waiting for transfers between devices, local(): gram = lax.psum(local_gram, ('dp', 'mp'))  241 us
    all_gather x1, waiting for transfers between devices, local(): feature_grad = jnp.sum(lax.all_gather(partial_grad, 'mp'), axis=0)  180 us
    gather x5, local copies, waits for them, and re-layouts, to_blocks(): jnp.take(tiled, order, axis=1).reshape(matrix.shape[0], block_count, -1)  18.5 us
    dot_general x7, matrix products, product(): return jnp.einsum('bij,bjk->bik', first, second, precision=highest)  13.5 us
    dot_general x1, matrix products, local(): lax.dot_general(cotangent, frozen_weight, (((1,), (1,)), ((), ())), prefe...  11.5 us
    reduce_sum x1, other arithmetic, local(): feature_grad = jnp.sum(lax.all_gather(partial_grad, 'mp'), axis=0)  11.2 us
  transfers between devices with their start and end apart: 2, of which 2 were waited for; matrix products, arithmetic and copies ran while one was open for 7% of the time, Pallas kernels for 0%

profile of v1, /device:TPU:2, one launch (start us, length us, event | category | flops | bytes accessed | tf_op | source)
XLA Modules:
  0.0 548.5 jit_solution(5337816072456594659)
XLA Ops:
  7.2 0.0 copy-start
  7.2 0.0 all-gather.3.cloned.1.call-start
  7.2 11.5 %fusion.34 = f32[512,2560]{1,0:T(8,128)} fusion(bf16[512,1728]{0,1:T(8,128)(2,1)} %param.7, bf16[2560,1728]{0,1:T(8,128)(2,1)} %param.8), kind=kOutput, calls=%fused_computation.62 | convolution fusion | flops 4529848320 | bytes 15859712 | tf_op jit(solution)/shard_map/dot_general | solution.py:54
  18.7 0.0 copy-start.5
  18.7 0.0 all-gather.3.cloned.1.call-update
  18.7 0.2 all-reduce.2.cloned.1.call-start
  19.0 0.4 copy-done.5
  19.4 0.1 broadcast_in_dim.63
  19.5 0.1 broadcast_in_dim.64
  19.6 2.5 copy.102
  22.1 0.0 copy-start.4
  22.1 2.8 copy.103
  24.9 0.0 copy-done.4
  24.9 0.2 reduce-window.8
  25.1 0.0 copy-done
  25.1 0.3 copy.124
  25.4 0.3 copy.109
  25.8 0.7 gather_fusion.3
  26.5 0.3 copy.110
  26.8 0.1 select_reduce_fusion
  26.9 0.1 compare_and_fusion.2
  27.0 0.5 bitcast_select_fusion
  27.5 2.4 bitcast_subtract_fusion
  29.9 3.9 fusion
  33.8 180.2 %all-gather.3.cloned.1.call-done = f32[2048,2560]{1,0:T(8,128)} async-done(((f32[512,2560]{1,0:T(8,128)}), f32[2048,2560]{1,0:T(8,128)}) %all-gather.3.cloned.1.call-update) | async-done | bytes 20971536 | tf_op jit(solution)/shard_map/all_gather | solution.py:57
  214.0 11.2 %reduce_sum.19 = f32[512,2560]{1,0:T(8,128)} reduce(f32[4,512,2560]{2,1,0:T(8,128)} %bitcast.49, f32[]{:T(128)} %constant.92.clone.1), dimensions={0}, to_apply=%region_1.2 | reduce | flops 3932160 | bytes 26214404 | tf_op jit(solution)/shard_map/reduce_sum | solution.py:57
  225.2 5.9 %copy.104 = f32[512,2560]{0,1:T(8,128)} copy(f32[512,2560]{1,0:T(8,128)} %reduce_sum.19) | data formatting | bytes 10485760 | tf_op jit(solution)/shard_map/reduce_sum | solution.py:57
  231.1 5.9 %copy.105 = f32[512,20,128]{2,0,1:T(8,128)} copy(f32[512,20,128]{0,2,1:T(8,128)} %bitcast.50) | data formatting | bytes 10485760 | tf_op jit(solution)/shard_map/reshape | solution.py:25
  237.0 5.7 %gather_fusion.1 = f32[20,512,128]{2,1,0:T(8,128)} fusion(f32[512,20,128]{2,0,1:T(8,128)} %copy.105, s32[1024]{0:T(1024)S(1)} %pad_clamp_fusion.1), kind=kCustom, calls=%fused_computation.1 | custom fusion | bytes 10485840 | tf_op jit(solution)/shard_map/jit(_take)/gather | solution.py:26
  242.7 5.9 %copy.106 = f32[512,20,128]{0,2,1:T(8,128)} copy(f32[512,20,128]{2,0,1:T(8,128)} %bitcast.48) | data formatting | bytes 10485760 | tf_op jit(solution)/shard_map/jit(_take)/gather | solution.py:26
  248.6 5.9 %copy.107 = f32[512,10,256]{2,0,1:T(8,128)} copy(f32[512,10,256]{0,2,1:T(8,128)} %bitcast.51) | data formatting | bytes 10485760 | tf_op jit(solution)/shard_map/jit(_take)/gather | solution.py:26
  254.6 2.9 broadcast_select_fusion
  257.5 0.0 copy-start.2
  257.5 2.3 copy-done.2
  259.8 2.8 fusion.11
  262.5 0.0 all-reduce.2.cloned.1.call-update
  262.6 1.5 copy.115
  264.1 2.9 fusion.33
  267.0 4.8 add_add_fusion
  271.8 3.2 gather_fusion
  274.9 3.2 gather_fusion.2
  278.1 4.7 fusion.7
  282.9 2.2 copy.122
  285.0 0.0 copy-start.3
  285.0 240.9 %all-reduce.2.cloned.1.call-done = f32[10,256,256]{2,1,0:T(8,128)} async-done(((f32[10,256,256]{2,1,0:T(8,128)}), f32[10,256,256]{2,1,0:T(8,128)}) %all-reduce.2.cloned.1.call-update) | async-done | bytes 2621456 | tf_op jit(solution)/shard_map/psum | solution.py:73
  525.9 4.8 fusion.2
  530.8 0.0 copy-done.3
  530.8 1.0 fusion.17
  531.9 1.0 fusion.19
  532.8 1.1 convolution_add_fusion.2
  534.0 0.9 convolution_add_fusion.1
  534.9 0.0 copy-start.1
  534.9 1.8 convolution_add_fusion
  536.7 2.3 copy.121
  539.0 1.5 fusion.14
  540.5 1.1 copy.123
  541.6 0.0 copy-done.1
  (10 shorter events, 0.1 us)
Async XLA Ops:
  7.2 17.9 %copy-start = (bf16[512,2560]{1,0:T(8,128)(2,1)S(1)}, bf16[512,2560]{1,0:T(8,128)(2,1)}, u32[]{:S(2)}) copy-start(bf16[512,2560]{1,0:T(8,128)(2,1)} %param.6) | copy-start | bytes 7864324
  7.2 206.8 %all-gather.3.cloned.1.call-start = ((), (), s32[]{:S(2)}) async-start(), calls=%async_computation.1 | async-start | bytes 26214400 | tf_op jit(solution)/shard_map/all_gather | solution.py:57
  18.7 0.7 copy-start.5
  18.7 507.2 %all-reduce.2.cloned.1.call-start = ((), (), s32[]{:S(2)}) async-start(), calls=%async_computation | async-start | bytes 5242880 | tf_op jit(solution)/shard_map/psum | solution.py:73
  22.1 2.8 copy-start.4
  257.5 2.3 copy-start.2
  285.0 245.8 %copy-start.3 = (f32[3,256,256]{2,0,1:T(4,128)S(1)}, f32[3,256,256]{2,0,1:T(4,128)}, u32[]{:S(2)}) copy-start(f32[3,256,256]{2,0,1:T(4,128)} %fusion) | copy-start | bytes 2359300
  534.9 6.7 %copy-start.1 = (bf16[512,2560]{1,0:T(8,128)(2,1)S(1)}, bf16[512,2560]{1,0:T(8,128)(2,1)}, u32[]{:S(2)}) copy-start(bf16[512,2560]{1,0:T(8,128)(2,1)} %param.6) | copy-start | bytes 7864324
Sparse Core Ops, SparseCore 0:
  18.9 195.0 all-gather.2
  262.7 263.1 all-reduce.1
